TPU v7x, 128 devices: a whole 4x4x4 slice. The times are simulated.
128 devices in a mesh: gx: 16 (over x, z_hi, core), gy: 8 (over z_lo, y).
Axes of the slice: x: 4, y: 4, z: 4 (z_hi: 2, z_lo: 2; z = z_hi * 2 + z_lo), core: 2. Of those that a mesh axis runs over, the one named last changes fastest.
Arguments:
- source_mass: float32 [32, 8, 8, 1024], P('gx', None, None, 'gy'), may hold values from 0.1 to 2
- alpha_start: float32 [32, 8, 8, 1024], P('gx', None, None, 'gy'), may hold values from -4 to 220
- part_start: float32 [32, 24, 24, 1024], P('gx', None, None, 'gy'), may hold values from 0.01 to 0.3
Outputs:
- alpha_final: float32 [32, 8, 8, 1024], P('gx', None, None, 'gy')
- partials_final: float32 [32, 24, 24, 1024], P('gx', None, None, 'gy')
All inputs are finite; a program needn't handle non-finite values.
Results may differ from a plain program's by a relative error of at most 0.00022.
Values sent between devices are 32-bit elements; how exact they have to be, the bound alone decides.
A program may use at most 64 MiB of HBM per device.

v0:
```python
import functools
import math

import jax
import jax.numpy as jnp
import ml_dtypes
import numpy as np
from jax import lax
from jax.experimental import pallas as pl
from jax.experimental.pallas import tpu as pltpu
from jax.sharding import PartitionSpec as P

ITERS = 2
LANES = 128
MESH = pl.DeviceIdType.MESH
LN2_HI = 0.693359375
LN2_LO = math.log(2.0) - 0.693359375
LOG2E = 1.0 / math.log(2.0)
F32 = jnp.float32
BF16 = jnp.bfloat16
EMPTY = -4000.0
TINY = 1.1754944e-38
N_HALO = 89
N_PACK = 113


def kernel_tables():
    a = np.arange(8)[:, None] + 8
    y = np.arange(24)[None, :]
    k1 = np.exp(-((a - y) ** 2) / 32.0)
    full = np.einsum("ay,bz->yzab", k1, k1).reshape(24, 3, 8, 64)
    full = full.transpose(1, 0, 2, 3)
    hi = full.astype(ml_dtypes.bfloat16)
    lo = (full - hi.astype(np.float64)).astype(ml_dtypes.bfloat16)
    forward = np.concatenate([hi, hi, lo], axis=3).reshape(576, 192)
    hi_rows = hi.reshape(3, 192, 64).transpose(0, 2, 1)
    lo_rows = lo.reshape(3, 192, 64).transpose(0, 2, 1)
    backward = np.concatenate([hi_rows, lo_rows], axis=1)
    return forward, backward


def roll_left(x):
    return pltpu.roll(x, LANES - 1, axis=x.ndim - 1)


def roll_right(x):
    return pltpu.roll(x, 1, axis=x.ndim - 1)


def lanes_of(shape):
    return lax.broadcasted_iota(jnp.int32, shape, len(shape) - 1)


def swap(x, first):
    return jnp.where(first, roll_left(x), roll_right(x))


def up8(x):
    return jnp.broadcast_to(x, (8, LANES))


def halves(x):
    hi = x.astype(BF16)
    lo = (x - hi.astype(F32)).astype(BF16)
    return hi, lo


def spread(u):
    hi, lo = halves(u)
    return jnp.concatenate([hi, lo, hi], axis=0)


def levels(e, ep, first, lam):
    sides = ((0,), (0, 1), (1,))
    ex, sh = [], []
    for part in range(3):
        own = [e[s] for s in sides[part]]
        both = own + [ep[s] for s in sides[part]]
        ex.append(functools.reduce(jnp.maximum, own))
        sh.append(functools.reduce(jnp.maximum, both))
    level = [
        [jnp.where(first, ex[p], sh[p]), sh[p], jnp.where(first, sh[p], ex[p])] for p in range(3)
    ]
    own_w, partner_w = [], []
    for p in range(3):
        own_w.append([[jnp.exp2(e[s] - level[p][b]) for b in range(3)] for s in sides[p]])
        rows = []
        for s in sides[p]:
            raw = [jnp.exp2(ep[s] - level[p][b]) for b in range(3)]
            rows.append([jnp.where(first, 0.0, raw[0]), raw[1], jnp.where(first, raw[2], 0.0)])
        partner_w.append(rows)
    if lam is None:
        new_e = [e[0], e[1]]
        lam_b = [[0.0] * 3 for _ in range(3)]
    else:
        lam_ex, lam_sh, lam_b = lam
        new_e = []
        for s, parts in ((0, (0, 1)), (1, (1, 2))):
            top = functools.reduce(
                jnp.maximum, [lam_ex[p] - ex[p] for p in parts] + [lam_sh[p] - sh[p] for p in parts]
            )
            new_e.append(-top)
    out_w, final_w = [], []
    for s, parts in ((0, (0, 1)), (1, (1, 2))):
        out_w.append(
            {p: [jnp.exp2(lam_b[p][b] - level[p][b] + new_e[s]) for b in range(3)] for p in parts}
        )
        final_w.append(
            {p: [jnp.exp2(e[s] - level[p][b] + lam_b[p][b]) for b in range(3)] for p in parts}
        )
    return own_w, partner_w, out_w, final_w, new_e, level


def region_scale(nu_ref, at, first):
    peak = []
    for part, (y0, y1) in enumerate(((0, 8), (8, 24), (24, 32))):
        row = []
        for b in range(3):
            top = jnp.max(nu_ref[b, y0:y1, :, at], axis=0)
            row.append(up8(jnp.max(top, axis=0, keepdims=True)))
        peak.append(row)

    def lg(x):
        exponent = jnp.floor(jnp.log(jnp.maximum(x, TINY)) * LOG2E)
        return jnp.where(x < TINY, EMPTY, exponent)

    lam_ex = [lg(jnp.where(first, peak[p][0], peak[p][2])) for p in range(3)]
    lam_sh = [
        lg(jnp.maximum(peak[p][1], jnp.where(first, peak[p][2], peak[p][0]))) for p in range(3)
    ]
    lam_b = [
        [
            jnp.where(first, lam_ex[p], lam_sh[p]),
            lam_sh[p],
            jnp.where(first, lam_sh[p], lam_ex[p]),
        ]
        for p in range(3)
    ]
    for part, (y0, y1) in enumerate(((0, 8), (8, 24), (24, 32))):
        for b in range(3):
            nu_ref[b, y0:y1, :, at] = nu_ref[b, y0:y1, :, at] * jnp.exp2(
                -jnp.maximum(lam_b[part][b], -125.0)
            )[None]
    return lam_ex, lam_sh, lam_b


def forward_sums(kf_ref, s_ref, side, u, up):
    cols = []
    for g in range(len(u)):
        cols += [u[g], up[g]]
    out = jnp.dot(
        kf_ref[...], spread(jnp.concatenate(cols, axis=1)), preferred_element_type=F32
    )
    s_ref[side, :, :, :, 0 : out.shape[1]] = out.reshape(3, 24, 8, out.shape[1])


def lanes_at(g):
    return slice(g * LANES, (g + 1) * LANES)


def ratio_rows(s_ref, nu_ref, g, chunk, b, own_w, partner_w, first):
    part = (0, 1, 1, 2)[chunk]
    sides = ((0,), (0, 1), (1,))[part]
    own_at, partner_at = lanes_at(2 * g), lanes_at(2 * g + 1)
    total = None
    for i, s in enumerate(sides):
        y0 = 8 * (chunk - s)
        own = s_ref[s, b, y0 : y0 + 8, :, own_at]
        if b == 1:
            partner = jnp.where(
                first[None],
                s_ref[s, 0, y0 : y0 + 8, :, partner_at],
                s_ref[s, 2, y0 : y0 + 8, :, partner_at],
            )
        else:
            partner = s_ref[s, 1, y0 : y0 + 8, :, partner_at]
        term = own * own_w[part][i][b][None] + partner * partner_w[part][i][b][None]
        total = term if total is None else total + term
    return nu_ref[b, 8 * chunk : 8 * chunk + 8, :, lanes_at(g)] / total


def backward(kb_ref, r_ref, s_ref, nu_ref, groups, weights, first, m):
    width = groups * LANES
    for g in range(groups):
        own_w, partner_w, out_w = weights[g][:3]
        for chunk in range(4):
            part = (0, 1, 1, 2)[chunk]
            for b in range(3):
                r = ratio_rows(s_ref, nu_ref, g, chunk, b, own_w, partner_w, first)
                for s in ((0,), (0, 1), (1,))[part]:
                    y0 = 8 * (chunk - s)
                    at = slice(s * width + g * LANES, s * width + (g + 1) * LANES)
                    r_ref[b, y0 : y0 + 8, :, at] = r * out_w[s][part][b][None]
    total = None
    for b in range(3):
        hi, lo = halves(r_ref[b, 0:24, :, 0 : 2 * width].reshape(192, 2 * width))
        top = jnp.dot(kb_ref[b], hi, preferred_element_type=F32)
        low = jnp.dot(kb_ref[b, 0:64, :], lo, preferred_element_type=F32)
        term = top[0:64] + (top[64:128] + low)
        total = term if total is None else total + term
    out = []
    for s in range(2):
        out.append(
            [
                m[s][g] / total[:, s * width + g * LANES : s * width + (g + 1) * LANES]
                for g in range(groups)
            ]
        )
    return out


def alpha_of(u, e):
    shape = u.shape
    e = jnp.broadcast_to(e[None], (shape[0] // 8, 8, LANES)).reshape(shape)
    return e * LN2_HI + (jnp.log(u) + e * LN2_LO)


def body(
    nx,
    ny,
    mass_ref,
    alpha_ref,
    part_ref,
    kf_ref,
    kb_ref,
    out_alpha_ref,
    out_part_ref,
    pu,
    pm,
    pq,
    pe,
    pack,
    gy_in,
    stage,
    s_ref,
    r_ref,
    nu_ref,
    e_ref,
    send_sem,
    recv_sem,
):
    gx = lax.axis_index("gx")
    gy = lax.axis_index("gy")
    core = lax.rem(gx, 2)
    near = (gx + 1 - 2 * core, gy)
    far = (lax.rem(gx + nx - 1 + 2 * core, nx), gy)
    before = (gx, lax.rem(gy + ny - 1, ny))
    after = (gx, lax.rem(gy + 1, ny))
    barrier = pltpu.get_barrier_semaphore()
    for target in (near, far, before, after):
        pl.semaphore_signal(barrier, inc=1, device_id=target, device_id_type=MESH)

    lane = lanes_of((8, LANES))
    odd = lax.rem(lane, 2) == 1
    even = jnp.logical_not(odd)
    edge = (lane == 0) | (lane == LANES - 1)

    phase_of = [jnp.where(core == c, 1, 0) for c in range(2)]
    u, e, m = [], [], []
    for c in range(2):
        alpha = alpha_ref[c]
        top = jnp.max(jnp.max(alpha, axis=0), axis=0, keepdims=True)
        level = up8(jnp.floor(top * LOG2E))
        u.append([jnp.exp((alpha - level[None] * LN2_HI) - level[None] * LN2_LO).reshape(64, LANES)])
        e.append(level)
        mass = mass_ref[c].reshape(64, LANES)
        m.append([mass])
        pm[phase_of[c], 1 - c] = mass
    for b in range(3):
        z = slice(8 * b, 8 * b + 8)
        for chunk in range(4):
            total = None
            for c in ((0,), (0, 1), (0, 1), (1,))[chunk]:
                y = slice(8 * (chunk - c), 8 * (chunk - c) + 8)
                term = part_ref[c, y, z, :]
                partner = part_ref[c, y, 8:16, :]
                if b == 1:
                    partner = jnp.where(even[None], part_ref[c, y, 0:8, :], part_ref[c, y, 16:24, :])
                total_own = term
                if b == 0:
                    source, mask = part_ref[c, y, 8:16, :], odd
                elif b == 2:
                    source, mask = part_ref[c, y, 8:16, :], even
                else:
                    source = jnp.where(even[None], part_ref[c, y, 16:24, :], part_ref[c, y, 0:8, :])
                    mask = None
                moved = swap(source, even[None])
                if mask is not None:
                    moved = jnp.where(mask[None], moved, 0.0)
                term = total_own + moved
                total = term if total is None else total + term
            nu_ref[b, 8 * chunk : 8 * chunk + 8, :, 0:LANES] = total
    ep = [swap(e[c], even) for c in range(2)]
    weights = [levels(e, ep, even, None)]
    for _ in range(ITERS):
        for c in range(2):
            forward_sums(kf_ref, s_ref, c, u[c], [swap(u[c][0], even[0:1])])
        u = backward(kb_ref, r_ref, s_ref, nu_ref, 1, weights, even, m)
    for c in range(2):
        forward_sums(kf_ref, s_ref, c, u[c], [swap(u[c][0], even[0:1])])
    own_w, partner_w, level = weights[0][0], weights[0][1], weights[0][5]
    for chunk in range(4):
        part = (0, 1, 1, 2)[chunk]
        for b in range(3):
            r = ratio_rows(s_ref, nu_ref, 0, chunk, b, own_w, partner_w, even)
            for c in ((0,), (0, 1), (1,))[part]:
                y0 = 8 * (chunk - c)
                root = jnp.exp2(0.5 * (e[c] - level[part][b]))[None]
                value = (s_ref[c, b, y0 : y0 + 8, :, 0:LANES] * root) * (r * root)
                stage[c, 24 * b + y0 : 24 * b + y0 + 8] = value
    for c in range(2):
        stage[c, 72:80] = u[c][0].reshape(8, 8, LANES)
        stage[c, 80:81] = e[c][None]
        stage[c, 81:89] = m[c][0].reshape(8, 8, LANES)
        low, mid, high = stage[c, 0:24], stage[c, 24:48], stage[c, 48:72]
        stage[c, 89:113] = jnp.where((lane == LANES - 1)[None], high, low)
        pu[phase_of[c], 1 - c, 0:64] = u[c][0]
        pu[phase_of[c], 1 - c, 64:72] = e[c]
        moved = swap(jnp.where(odd[None], high, low), odd[None])
        mid = mid + jnp.where(edge[None], 0.0, moved)
        pq[phase_of[c], 1 - c, 0] = jnp.where(odd[None], low, mid)
        pq[phase_of[c], 1 - c, 1] = jnp.where(odd[None], mid, high)

    def pack_step(i, held):
        out = []
        for c in range(2):
            for half in range(2):
                x = stage[c, half * 64 + i]
                x = pltpu.roll(x, 2 * i + 1, axis=1)
                out.append(jnp.where(lax.div(lane, 2) == i, x, held[2 * c + half]))
        return tuple(out)

    for c in range(2):
        stage[c, 113:128] = jnp.zeros((15, 8, LANES), F32)
    zero = jnp.zeros((8, LANES), F32)
    packed = lax.fori_loop(0, 64, pack_step, (zero, zero, zero, zero))
    for c in range(2):
        for half in range(2):
            pack[c, half] = packed[2 * c + half]

    pl.semaphore_wait(barrier, 4)

    def copy(src, dst, sem, target):
        return pltpu.make_async_remote_copy(
            src_ref=src,
            dst_ref=dst,
            send_sem=send_sem.at[sem],
            recv_sem=recv_sem.at[sem],
            device_id=target,
            device_id_type=MESH,
        )

    near_side, far_side = core, 1 - core
    to_before = copy(pack, gy_in.at[1], 0, before)
    to_after = copy(pack, gy_in.at[0], 1, after)
    to_before.start()
    to_after.start()
    sends = {}
    for name, phase, side, target, sem in (
        ("far", 1, far_side, far, 2),
        ("near", 0, near_side, near, 6),
    ):
        for i, buf in enumerate((pu, pq, pm)):
            where = buf.at[phase, side]
            sends[name, i] = copy(where, where, sem + i, target)
            sends[name, i].start()
        where = pe.at[phase, side]
        sends[name, 3] = copy(where, where, sem + 3, target)
    to_before.wait()
    to_after.wait()
    own_entry = (lane >= 2 * (N_HALO - 64))
    for c in range(2):
        for half in range(2):
            merged = jnp.where(even, gy_in[0, c, half], gy_in[1, c, half])
            if half == 1:
                merged = jnp.where(own_entry, pack[c, half], merged)
            pe[phase_of[c], 1 - c, half] = merged
    sends["near", 3].start()
    sends["far", 3].start()

    for phase, name in ((0, "near"), (1, "far")):
        for i in range(4):
            sends[name, i].wait()
        own_side = near_side if phase == 0 else far_side

        def unpack_step(i, _):
            for side in range(2):
                for half in range(2):
                    shift = LANES - (2 * i + 1)
                    stage[side, half * 64 + i] = pltpu.roll(pe[phase, side, half], shift, axis=1)
            return 0

        lax.fori_loop(0, 64, unpack_step, 0)

        for chunk in range(4):
            sides = ((0,), (0, 1), (0, 1), (1,))[chunk]

            def both(read):
                total = None
                for s in sides:
                    term = read(s, 8 * (chunk - s))
                    total = term if total is None else total + term
                return total

            low = both(lambda s, y: pq[phase, s, 0, y : y + 8])
            high = both(lambda s, y: pq[phase, s, 1, y : y + 8])
            ep0, ep1, ep2 = [
                both(lambda s, y, b=b: stage[s, 24 * b + y : 24 * b + y + 8]) for b in range(3)
            ]
            kept = both(lambda s, y: stage[s, 89 + y : 89 + y + 8])
            moved = swap(jnp.where(odd[None], ep2, ep0), odd[None])
            low = low + jnp.where((lane == 0)[None], moved, 0.0)
            high = high + jnp.where((lane == LANES - 1)[None], moved, 0.0)
            other = swap(jnp.where(odd[None], high, low), odd[None])
            other = jnp.where(edge[None], kept + swap(ep1, odd[None]), other)
            rows = slice(8 * chunk, 8 * chunk + 8)
            main, outer = lanes_at(0), lanes_at(1)
            nu_ref[0, rows, :, main] = jnp.where(odd[None], low, other)
            nu_ref[1, rows, :, main] = jnp.where(odd[None], high, low)
            nu_ref[2, rows, :, main] = jnp.where(odd[None], other, high)
            nu_ref[0, rows, :, outer] = jnp.where(odd[None], ep0, swap(high, odd[None]))
            nu_ref[1, rows, :, outer] = swap(other, odd[None])
            nu_ref[2, rows, :, outer] = jnp.where(odd[None], swap(low, odd[None]), ep2)

        u = [[pu[phase, s, 0:64], stage[s, 72:80].reshape(64, LANES)] for s in range(2)]
        e = [[pu[phase, s, 64:72], stage[s, 80]] for s in range(2)]
        m = [[pm[phase, s], stage[s, 81:89].reshape(64, LANES)] for s in range(2)]
        lam = [region_scale(nu_ref, lanes_at(g), odd) for g in range(2)]

        def partners(x, mask, at_edge):
            moved_main, moved_edge = swap(x[0], mask), swap(x[1], mask)
            return [jnp.where(at_edge, moved_edge, moved_main), moved_main]

        for it in range(ITERS + 1):
            for s in range(2):
                forward_sums(kf_ref, s_ref, s, u[s], partners(u[s], odd[0:1], edge[0:1]))
            ep = [partners(e[s], odd, edge) for s in range(2)]
            weights = [
                levels([e[0][g], e[1][g]], [ep[0][g], ep[1][g]], odd, lam[g]) for g in range(2)
            ]
            if it < ITERS:
                u = backward(kb_ref, r_ref, s_ref, nu_ref, 2, weights, odd, m)
                e = [[weights[g][4][s] for g in range(2)] for s in range(2)]

        own_w, partner_w, _, final_w = weights[0][:4]
        own_col = 1 - own_side
        for chunk in range(4):
            for b in range(3):
                r_ref[b, 8 * chunk : 8 * chunk + 8, :, 0:LANES] = ratio_rows(
                    s_ref, nu_ref, 0, chunk, b, own_w, partner_w, odd
                )
        for b in range(3):
            e_ref[0, b] = final_w[0][0][b]
            e_ref[1, b] = final_w[0][1][b]
            e_ref[2, b] = final_w[0][1][b]
            e_ref[3, b] = final_w[1][1][b]
            e_ref[4, b] = final_w[1][1][b]
            e_ref[5, b] = final_w[1][2][b]
        for k in range(3):
            for b in range(3):
                r = r_ref[b, pl.ds(8 * (k + own_side), 8), :, 0:LANES]
                scale = e_ref[3 * own_side + k, b]
                sums = s_ref[own_side, b, 8 * k : 8 * k + 8, :, 0:LANES]
                out_part_ref[own_col, 8 * k : 8 * k + 8, 8 * b : 8 * b + 8, :] = sums * (
                    r * scale[None]
                )
        left = (own_side == 0)
        own_u = jnp.where(left, u[0][0], u[1][0])
        own_e = jnp.where(left, e[0][0], e[1][0])
        out_alpha_ref[own_col] = alpha_of(own_u, own_e).reshape(8, 8, LANES)


def per_device(nx, ny, source_mass, alpha_start, part_start):
    forward, back = kernel_tables()
    vmem = pl.BlockSpec(memory_space=pltpu.VMEM)
    return pl.pallas_call(
        functools.partial(body, nx, ny),
        out_shape=(
            jax.ShapeDtypeStruct(alpha_start.shape, F32),
            jax.ShapeDtypeStruct(part_start.shape, F32),
        ),
        in_specs=[vmem] * 5,
        out_specs=(vmem, vmem),
        scratch_shapes=[
            pltpu.VMEM((2, 2, 72, LANES), F32),
            pltpu.VMEM((2, 2, 64, LANES), F32),
            pltpu.VMEM((2, 2, 2, 24, 8, LANES), F32),
            pltpu.VMEM((2, 2, 2, 8, LANES), F32),
            pltpu.VMEM((2, 2, 8, LANES), F32),
            pltpu.VMEM((2, 2, 2, 8, LANES), F32),
            pltpu.VMEM((2, 128, 8, LANES), F32),
            pltpu.VMEM((2, 3, 24, 8, 4 * LANES), F32),
            pltpu.VMEM((3, 32, 8, 4 * LANES), F32),
            pltpu.VMEM((3, 32, 8, 2 * LANES), F32),
            pltpu.VMEM((6, 3, 8, LANES), F32),
            pltpu.SemaphoreType.DMA((10,)),
            pltpu.SemaphoreType.DMA((10,)),
        ],
        compiler_params=pltpu.CompilerParams(
            collective_id=0, has_side_effects=True, vmem_limit_bytes=48 * 2**20
        ),
    )(source_mass, alpha_start, part_start, jnp.asarray(forward), jnp.asarray(back))


def solution(mesh):
    placed = P("gx", None, None, "gy")
    return jax.shard_map(
        functools.partial(per_device, mesh.shape["gx"], mesh.shape["gy"]),
        mesh=mesh,
        in_specs=(placed, placed, placed),
        out_specs=(placed, placed),
        check_vma=False,
    )
```

profile of v0, /device:TPU:1, one launch (start us, length us, event | category | flops | bytes accessed | tf_op | source)
XLA Modules:
  0.0 36.9 jit_solution(11884110462059156961)
XLA Ops:
  0.6 0.0 copy-start
  0.6 1.1 %copy-done = f32[2,24,24,128]{3,2,1,0:T(8,128)S(1)} copy-done((f32[2,24,24,128]{3,2,1,0:T(8,128)S(1)}, f32[2,24,24,128]{3,2,1,0:T(8,128)}, u32[]{:S(2)}) %copy-start) | copy-done | bytes 589848
  1.7 0.0 copy-start.1
  1.7 1.0 %copy-done.1 = bf16[576,192]{1,0:T(8,128)(2,1)S(1)} copy-done((bf16[576,192]{1,0:T(8,128)(2,1)S(1)}, bf16[576,192]{1,0:T(8,128)(2,1)}, u32[]{:S(2)}) %copy-start.1) | copy-done | bytes 221208
  2.7 0.0 copy-start.2
  2.7 0.9 %copy-done.2 = bf16[3,128,192]{2,1,0:T(8,128)(2,1)S(1)} copy-done((bf16[3,128,192]{2,1,0:T(8,128)(2,1)S(1)}, bf16[3,128,192]{2,1,0:T(8,128)(2,1)}, u32[]{:S(2)}) %copy-start.2) | copy-done | bytes 147480
  3.6 0.0 copy-start.3
  3.6 0.8 %copy-done.3 = f32[2,8,8,128]{3,2,1,0:T(8,128)S(1)} copy-done((f32[2,8,8,128]{3,2,1,0:T(8,128)S(1)}, f32[2,8,8,128]{3,2,1,0:T(8,128)}, u32[]{:S(2)}) %copy-start.3) | copy-done | bytes 65560
  4.4 0.0 copy-start.4
  4.4 0.8 %copy-done.4 = f32[2,8,8,128]{3,2,1,0:T(8,128)S(1)} copy-done((f32[2,8,8,128]{3,2,1,0:T(8,128)S(1)}, f32[2,8,8,128]{3,2,1,0:T(8,128)}, u32[]{:S(2)}) %copy-start.4) | copy-done | bytes 65560
  5.3 30.2 %shard_map.68 = (f32[2,8,8,128]{3,2,1,0:T(8,128)S(1)}, f32[2,24,24,128]{3,2,1,0:T(8,128)S(1)}) custom-call(f32[2,8,8,128]{3,2,1,0:T(8,128)S(1)} %copy-done.3, f32[2,8,8,128]{3,2,1,0:T(8,128)S(1)} %copy-done.4, f32[2,24,24,128]{3,2,1,0:T(8,128)S(1)} %copy-done, bf16[576,192]{1,0:T(8,128)(2,1)S(1)} %copy-done.1, bf16[3,128,192]{2,1,0:T(8,128)(2,1)S(1)} %copy-done.2), custom_call_target="tpu_custom_call" | custom-call | tf_op jit(solution)/shard_map/pallas_call | solution.py:476
  35.5 0.6 %copy.9 = f32[2,8,8,128]{3,2,1,0:T(8,128)} copy(f32[2,8,8,128]{3,2,1,0:T(8,128)S(1)} %get-tuple-element.4) | data formatting | bytes 131072
  36.1 0.8 %copy.10 = f32[2,24,24,128]{3,2,1,0:T(8,128)} copy(f32[2,24,24,128]{3,2,1,0:T(8,128)S(1)} %get-tuple-element.5) | data formatting | bytes 1179648
Async XLA Ops:
  0.6 1.1 %copy-start = (f32[2,24,24,128]{3,2,1,0:T(8,128)S(1)}, f32[2,24,24,128]{3,2,1,0:T(8,128)}, u32[]{:S(2)}) copy-start(f32[2,24,24,128]{3,2,1,0:T(8,128)} %part_ref.1) | copy-start | bytes 1769476
  1.7 1.0 %copy-start.1 = (bf16[576,192]{1,0:T(8,128)(2,1)S(1)}, bf16[576,192]{1,0:T(8,128)(2,1)}, u32[]{:S(2)}) copy-start(bf16[576,192]{1,0:T(8,128)(2,1)} %constant.4.clone.kf_ref) | copy-start | bytes 663556
  2.7 0.9 %copy-start.2 = (bf16[3,128,192]{2,1,0:T(8,128)(2,1)S(1)}, bf16[3,128,192]{2,1,0:T(8,128)(2,1)}, u32[]{:S(2)}) copy-start(bf16[3,128,192]{2,1,0:T(8,128)(2,1)} %constant.5.clone.kb_ref) | copy-start | bytes 442372
  3.6 0.8 %copy-start.3 = (f32[2,8,8,128]{3,2,1,0:T(8,128)S(1)}, f32[2,8,8,128]{3,2,1,0:T(8,128)}, u32[]{:S(2)}) copy-start(f32[2,8,8,128]{3,2,1,0:T(8,128)} %mass_ref.1) | copy-start | bytes 196612
  4.4 0.8 %copy-start.4 = (f32[2,8,8,128]{3,2,1,0:T(8,128)S(1)}, f32[2,8,8,128]{3,2,1,0:T(8,128)}, u32[]{:S(2)}) copy-start(f32[2,8,8,128]{3,2,1,0:T(8,128)} %alpha_ref.1) | copy-start | bytes 196612
where the time goes:
time: 37.2 us; the launch traced here: 36.9 us
  Pallas kernels  30.2 us (81%)
  local copies, waits for them, and re-layouts  6.07 us (16%)
  between operations  0.65 us (2%)
    pallas_call x1, Pallas kernels, per_device(): pl.pallas_call(functools.partial(body, nx, ny), out_shape=(jax.ShapeDtype...  30.2 us
    unnamed x12, local copies, waits for them, and re-layouts  6.07 us

commit v1 on v0

--- a/solution.py
+++ b/solution.py
@@ -218,11 +218,11 @@
 def body(
     nx,
     ny,
-    mass_ref,
-    alpha_ref,
-    part_ref,
-    kf_ref,
-    kb_ref,
+    mass_hbm,
+    alpha_hbm,
+    part_hbm,
+    kf_hbm,
+    kb_hbm,
     out_alpha_ref,
     out_part_ref,
     pu,
@@ -236,6 +236,12 @@
     r_ref,
     nu_ref,
     e_ref,
+    mass_ref,
+    alpha_ref,
+    part_ref,
+    kf_ref,
+    kb_ref,
+    load_sem,
     send_sem,
     recv_sem,
 ):
@@ -250,6 +256,21 @@
     for target in (near, far, before, after):
         pl.semaphore_signal(barrier, inc=1, device_id=target, device_id_type=MESH)
 
+    loads = [
+        pltpu.make_async_copy(src, dst, load_sem.at[i])
+        for i, (src, dst) in enumerate(
+            (
+                (alpha_hbm, alpha_ref),
+                (mass_hbm, mass_ref),
+                (part_hbm, part_ref),
+                (kf_hbm, kf_ref),
+                (kb_hbm, kb_ref),
+            )
+        )
+    ]
+    for load in loads:
+        load.start()
+
     lane = lanes_of((8, LANES))
     odd = lax.rem(lane, 2) == 1
     even = jnp.logical_not(odd)
@@ -257,6 +278,8 @@
 
     phase_of = [jnp.where(core == c, 1, 0) for c in range(2)]
     u, e, m = [], [], []
+    loads[0].wait()
+    loads[1].wait()
     for c in range(2):
         alpha = alpha_ref[c]
         top = jnp.max(jnp.max(alpha, axis=0), axis=0, keepdims=True)
@@ -266,6 +289,7 @@
         mass = mass_ref[c].reshape(64, LANES)
         m.append([mass])
         pm[phase_of[c], 1 - c] = mass
+    loads[2].wait()
     for b in range(3):
         z = slice(8 * b, 8 * b + 8)
         for chunk in range(4):
@@ -292,6 +316,8 @@
             nu_ref[b, 8 * chunk : 8 * chunk + 8, :, 0:LANES] = total
     ep = [swap(e[c], even) for c in range(2)]
     weights = [levels(e, ep, even, None)]
+    loads[3].wait()
+    loads[4].wait()
     for _ in range(ITERS):
         for c in range(2):
             forward_sums(kf_ref, s_ref, c, u[c], [swap(u[c][0], even[0:1])])
@@ -333,7 +359,7 @@
     for c in range(2):
         stage[c, 113:128] = jnp.zeros((15, 8, LANES), F32)
     zero = jnp.zeros((8, LANES), F32)
-    packed = lax.fori_loop(0, 64, pack_step, (zero, zero, zero, zero))
+    packed = lax.fori_loop(0, 64, pack_step, (zero, zero, zero, zero), unroll=16)
     for c in range(2):
         for half in range(2):
             pack[c, half] = packed[2 * c + half]
@@ -390,7 +416,7 @@
                     stage[side, half * 64 + i] = pltpu.roll(pe[phase, side, half], shift, axis=1)
             return 0
 
-        lax.fori_loop(0, 64, unpack_step, 0)
+        lax.fori_loop(0, 64, unpack_step, 0, unroll=16)
 
         for chunk in range(4):
             sides = ((0,), (0, 1), (0, 1), (1,))[chunk]
@@ -479,7 +505,7 @@
             jax.ShapeDtypeStruct(alpha_start.shape, F32),
             jax.ShapeDtypeStruct(part_start.shape, F32),
         ),
-        in_specs=[vmem] * 5,
+        in_specs=[pl.BlockSpec(memory_space=pl.ANY)] * 5,
         out_specs=(vmem, vmem),
         scratch_shapes=[
             pltpu.VMEM((2, 2, 72, LANES), F32),
@@ -493,6 +519,12 @@
             pltpu.VMEM((3, 32, 8, 4 * LANES), F32),
             pltpu.VMEM((3, 32, 8, 2 * LANES), F32),
             pltpu.VMEM((6, 3, 8, LANES), F32),
+            pltpu.VMEM(source_mass.shape, F32),
+            pltpu.VMEM(alpha_start.shape, F32),
+            pltpu.VMEM(part_start.shape, F32),
+            pltpu.VMEM(forward.shape, BF16),
+            pltpu.VMEM(back.shape, BF16),
+            pltpu.SemaphoreType.DMA((5,)),
             pltpu.SemaphoreType.DMA((10,)),
             pltpu.SemaphoreType.DMA((10,)),
         ],

time: 37.2 us -> 27 us (0.73)
  Pallas kernels: 30.2 us -> 20 us
    pallas_call x1, Pallas kernels: 30.2 us -> 20 us  [per_device(): pl.pallas_call(functools.partial(body, nx, ny), out_shape=(jax.ShapeDtype...]
where the time goes in v1:
time: 27 us; the launch traced here: 26.7 us
  Pallas kernels  20 us (74%)
  local copies, waits for them, and re-layouts  6.07 us (22%)
  between operations  0.65 us (2%)
    pallas_call x1, Pallas kernels, per_device(): pl.pallas_call(functools.partial(body, nx, ny), out_shape=(jax.ShapeDtype...  20 us
    unnamed x12, local copies, waits for them, and re-layouts  6.07 us

profile of v1, /device:TPU:1, one launch (start us, length us, event | category | flops | bytes accessed | tf_op | source)
XLA Modules:
  0.0 26.7 jit_solution(5163807498875231324)
XLA Ops:
  0.6 0.0 copy-start
  0.6 1.1 %copy-done = f32[2,24,24,128]{3,2,1,0:T(8,128)S(1)} copy-done((f32[2,24,24,128]{3,2,1,0:T(8,128)S(1)}, f32[2,24,24,128]{3,2,1,0:T(8,128)}, u32[]{:S(2)}) %copy-start) | copy-done | bytes 589848
  1.7 0.0 copy-start.1
  1.7 1.0 %copy-done.1 = bf16[576,192]{1,0:T(8,128)(2,1)S(1)} copy-done((bf16[576,192]{1,0:T(8,128)(2,1)S(1)}, bf16[576,192]{1,0:T(8,128)(2,1)}, u32[]{:S(2)}) %copy-start.1) | copy-done | bytes 221208
  2.7 0.0 copy-start.2
  2.7 0.9 %copy-done.2 = bf16[3,128,192]{2,1,0:T(8,128)(2,1)S(1)} copy-done((bf16[3,128,192]{2,1,0:T(8,128)(2,1)S(1)}, bf16[3,128,192]{2,1,0:T(8,128)(2,1)}, u32[]{:S(2)}) %copy-start.2) | copy-done | bytes 147480
  3.6 0.0 copy-start.3
  3.6 0.8 %copy-done.3 = f32[2,8,8,128]{3,2,1,0:T(8,128)S(1)} copy-done((f32[2,8,8,128]{3,2,1,0:T(8,128)S(1)}, f32[2,8,8,128]{3,2,1,0:T(8,128)}, u32[]{:S(2)}) %copy-start.3) | copy-done | bytes 65560
  4.4 0.0 copy-start.4
  4.4 0.8 %copy-done.4 = f32[2,8,8,128]{3,2,1,0:T(8,128)S(1)} copy-done((f32[2,8,8,128]{3,2,1,0:T(8,128)S(1)}, f32[2,8,8,128]{3,2,1,0:T(8,128)}, u32[]{:S(2)}) %copy-start.4) | copy-done | bytes 65560
  5.3 20.0 %shard_map.68 = (f32[2,8,8,128]{3,2,1,0:T(8,128)S(1)}, f32[2,24,24,128]{3,2,1,0:T(8,128)S(1)}) custom-call(f32[2,8,8,128]{3,2,1,0:T(8,128)S(1)} %copy-done.3, f32[2,8,8,128]{3,2,1,0:T(8,128)S(1)} %copy-done.4, f32[2,24,24,128]{3,2,1,0:T(8,128)S(1)} %copy-done, bf16[576,192]{1,0:T(8,128)(2,1)S(1)} %copy-done.1, bf16[3,128,192]{2,1,0:T(8,128)(2,1)S(1)} %copy-done.2), custom_call_target="tpu_custom_call" | custom-call | tf_op jit(solution)/shard_map/pallas_call | solution.py:502
  25.3 0.6 %copy.9 = f32[2,8,8,128]{3,2,1,0:T(8,128)} copy(f32[2,8,8,128]{3,2,1,0:T(8,128)S(1)} %get-tuple-element.4) | data formatting | bytes 131072
  25.9 0.8 %copy.10 = f32[2,24,24,128]{3,2,1,0:T(8,128)} copy(f32[2,24,24,128]{3,2,1,0:T(8,128)S(1)} %get-tuple-element.5) | data formatting | bytes 1179648
Async XLA Ops:
  0.6 1.1 %copy-start = (f32[2,24,24,128]{3,2,1,0:T(8,128)S(1)}, f32[2,24,24,128]{3,2,1,0:T(8,128)}, u32[]{:S(2)}) copy-start(f32[2,24,24,128]{3,2,1,0:T(8,128)} %part_hbm.1) | copy-start | bytes 1769476
  1.7 1.0 %copy-start.1 = (bf16[576,192]{1,0:T(8,128)(2,1)S(1)}, bf16[576,192]{1,0:T(8,128)(2,1)}, u32[]{:S(2)}) copy-start(bf16[576,192]{1,0:T(8,128)(2,1)} %constant.4.clone.kf_hbm) | copy-start | bytes 663556
  2.7 0.9 %copy-start.2 = (bf16[3,128,192]{2,1,0:T(8,128)(2,1)S(1)}, bf16[3,128,192]{2,1,0:T(8,128)(2,1)}, u32[]{:S(2)}) copy-start(bf16[3,128,192]{2,1,0:T(8,128)(2,1)} %constant.5.clone.kb_hbm) | copy-start | bytes 442372
  3.6 0.8 %copy-start.3 = (f32[2,8,8,128]{3,2,1,0:T(8,128)S(1)}, f32[2,8,8,128]{3,2,1,0:T(8,128)}, u32[]{:S(2)}) copy-start(f32[2,8,8,128]{3,2,1,0:T(8,128)} %mass_hbm.1) | copy-start | bytes 196612
  4.4 0.8 %copy-start.4 = (f32[2,8,8,128]{3,2,1,0:T(8,128)S(1)}, f32[2,8,8,128]{3,2,1,0:T(8,128)}, u32[]{:S(2)}) copy-start(f32[2,8,8,128]{3,2,1,0:T(8,128)} %alpha_hbm.1) | copy-start | bytes 196612

commit v2 on v1

--- a/solution.py
+++ b/solution.py
@@ -496,16 +496,26 @@
         out_alpha_ref[own_col] = alpha_of(own_u, own_e).reshape(8, 8, LANES)
 
 
+def write_out(alpha_in, part_in, alpha_out, part_out, sem):
+    copies = [pltpu.make_async_copy(alpha_in, alpha_out, sem.at[0])]
+    for c in range(2):
+        copies.append(pltpu.make_async_copy(part_in.at[c], part_out.at[c], sem.at[1 + c]))
+    for copy in copies:
+        copy.start()
+    for copy in copies:
+        copy.wait()
+
+
 def per_device(nx, ny, source_mass, alpha_start, part_start):
     forward, back = kernel_tables()
     vmem = pl.BlockSpec(memory_space=pltpu.VMEM)
-    return pl.pallas_call(
+    results = pl.pallas_call(
         functools.partial(body, nx, ny),
         out_shape=(
-            jax.ShapeDtypeStruct(alpha_start.shape, F32),
-            jax.ShapeDtypeStruct(part_start.shape, F32),
+            pltpu.VMEM(alpha_start.shape, F32),
+            pltpu.VMEM(part_start.shape, F32),
         ),
-        in_specs=[pl.BlockSpec(memory_space=pl.ANY)] * 5,
+        in_specs=[pl.BlockSpec(memory_space=pltpu.HBM)] * 5,
         out_specs=(vmem, vmem),
         scratch_shapes=[
             pltpu.VMEM((2, 2, 72, LANES), F32),
@@ -529,9 +539,21 @@
             pltpu.SemaphoreType.DMA((10,)),
         ],
         compiler_params=pltpu.CompilerParams(
-            collective_id=0, has_side_effects=True, vmem_limit_bytes=48 * 2**20
+            collective_id=0, has_side_effects=True, vmem_limit_bytes=56 * 2**20
         ),
-    )(source_mass, alpha_start, part_start, jnp.asarray(forward), jnp.asarray(back))
+    )(*[
+        pltpu.with_memory_space_constraint(x, pltpu.HBM)
+        for x in (source_mass, alpha_start, part_start, jnp.asarray(forward), jnp.asarray(back))
+    ])
+    anywhere = pl.BlockSpec(memory_space=pl.ANY)
+    return pl.pallas_call(
+        write_out,
+        out_shape=tuple(jax.ShapeDtypeStruct(r.shape, r.dtype) for r in results),
+        in_specs=[vmem] * 2,
+        out_specs=(anywhere, anywhere),
+        scratch_shapes=[pltpu.SemaphoreType.DMA((3,))],
+        compiler_params=pltpu.CompilerParams(vmem_limit_bytes=16 * 2**20),
+    )(*results)
 
 
 def solution(mesh):

time: 27 us -> 22 us (0.81)
  local copies, waits for them, and re-layouts: 6.07 us -> 0 us
  Pallas kernels: 20 us -> 21.2 us
    unnamed x12 -> x0, local copies, waits for them, and re-layouts: 6.07 us -> none
    pallas_call x1 -> x2, Pallas kernels: 20 us -> 21.2 us  [the longest x1 20.4 us: per_device(): pl.pallas_call(functools.partial(body, nx, ny), out_shape=(pltpu.VMEM(alp...]
where the time goes in v2:
time: 22 us; the launch traced here: 21.9 us
  Pallas kernels  21.2 us (96%)
  between operations  0.64 us (3%)
    pallas_call x1, Pallas kernels, per_device(): pl.pallas_call(functools.partial(body, nx, ny), out_shape=(pltpu.VMEM(alp...  20.4 us
    pallas_call x1, Pallas kernels, per_device(): pl.pallas_call(write_out, out_shape=tuple((jax.ShapeDtypeStruct(r.shape,...  0.86 us

profile of v2, /device:TPU:1, one launch (start us, length us, event | category | flops | bytes accessed | tf_op | source)
XLA Modules:
  0.0 21.9 jit_solution(861210371532503682)
XLA Ops:
  0.6 20.4 %shard_map.68 = (f32[2,8,8,128]{3,2,1,0:T(8,128)S(1)}, f32[2,24,24,128]{3,2,1,0:T(8,128)S(1)}) custom-call(f32[2,8,8,128]{3,2,1,0:T(8,128)} %mass_hbm.1, f32[2,8,8,128]{3,2,1,0:T(8,128)} %alpha_hbm.1, f32[2,24,24,128]{3,2,1,0:T(8,128)} %part_hbm.1, bf16[576,192]{1,0:T(8,128)(2,1)} %constant.4.clone.kf_hbm, bf16[3,128,192]{2,1,0:T(8,128)(2,1)} %constant.5.clone.kb_hbm), custom_call_target="tpu_custom_call" | custom-call | tf_op jit(solution)/shard_map/pallas_call | solution.py:512
  21.0 0.9 %shard_map.69 = (f32[2,8,8,128]{3,2,1,0:T(8,128)}, f32[2,24,24,128]{3,2,1,0:T(8,128)}) custom-call(f32[2,8,8,128]{3,2,1,0:T(8,128)S(1)} %get-tuple-element.4.alpha_in, f32[2,24,24,128]{3,2,1,0:T(8,128)S(1)} %get-tuple-element.5.part_in), custom_call_target="tpu_custom_call" | custom-call | tf_op jit(solution)/shard_map/pallas_call | solution.py:549

commit v3 on v2

--- a/solution.py
+++ b/solution.py
@@ -179,7 +179,7 @@
     return nu_ref[b, 8 * chunk : 8 * chunk + 8, :, lanes_at(g)] / total
 
 
-def backward(kb_ref, r_ref, s_ref, nu_ref, groups, weights, first, m):
+def source_sums(kb_ref, r_ref, s_ref, nu_ref, groups, weights, first):
     width = groups * LANES
     for g in range(groups):
         own_w, partner_w, out_w = weights[g][:3]
@@ -198,15 +198,17 @@
         low = jnp.dot(kb_ref[b, 0:64, :], lo, preferred_element_type=F32)
         term = top[0:64] + (top[64:128] + low)
         total = term if total is None else total + term
-    out = []
-    for s in range(2):
-        out.append(
-            [
-                m[s][g] / total[:, s * width + g * LANES : s * width + (g + 1) * LANES]
-                for g in range(groups)
-            ]
-        )
-    return out
+    return [
+        [
+            total[:, s * width + g * LANES : s * width + (g + 1) * LANES]
+            for g in range(groups)
+        ]
+        for s in range(2)
+    ]
+
+
+def new_potential(total, m):
+    return [[m[s][g] / total[s][g] for g in range(len(m[s]))] for s in range(2)]
 
 
 def alpha_of(u, e):
@@ -321,7 +323,37 @@
     for _ in range(ITERS):
         for c in range(2):
             forward_sums(kf_ref, s_ref, c, u[c], [swap(u[c][0], even[0:1])])
-        u = backward(kb_ref, r_ref, s_ref, nu_ref, 1, weights, even, m)
+        u = new_potential(source_sums(kb_ref, r_ref, s_ref, nu_ref, 1, weights, even), m)
+    for c in range(2):
+        pu[phase_of[c], 1 - c, 0:64] = u[c][0]
+        pu[phase_of[c], 1 - c, 64:72] = e[c]
+
+    def copy(src, dst, sem, target):
+        return pltpu.make_async_remote_copy(
+            src_ref=src,
+            dst_ref=dst,
+            send_sem=send_sem.at[sem],
+            recv_sem=recv_sem.at[sem],
+            device_id=target,
+            device_id_type=MESH,
+        )
+
+    to_before = copy(pack, gy_in.at[1], 0, before)
+    to_after = copy(pack, gy_in.at[0], 1, after)
+    near_side, far_side = core, 1 - core
+    sends = {}
+    for name, phase, side, target in (("far", 1, far_side, far), ("near", 0, near_side, near)):
+        for i, (key, where) in enumerate(
+            (
+                ("potential", pu.at[phase, side]),
+                ("low", pq.at[phase, side, 0]),
+                ("high", pq.at[phase, side, 1]),
+                ("edges", pe.at[phase, side]),
+                ("mass", pm.at[phase, side]),
+            )
+        ):
+            sends[name, key] = copy(where, where, 2 + 5 * phase + i, target)
+
     for c in range(2):
         forward_sums(kf_ref, s_ref, c, u[c], [swap(u[c][0], even[0:1])])
     own_w, partner_w, level = weights[0][0], weights[0][1], weights[0][5]
@@ -335,89 +367,70 @@
                 value = (s_ref[c, b, y0 : y0 + 8, :, 0:LANES] * root) * (r * root)
                 stage[c, 24 * b + y0 : 24 * b + y0 + 8] = value
     for c in range(2):
-        stage[c, 72:80] = u[c][0].reshape(8, 8, LANES)
-        stage[c, 80:81] = e[c][None]
-        stage[c, 81:89] = m[c][0].reshape(8, 8, LANES)
         low, mid, high = stage[c, 0:24], stage[c, 24:48], stage[c, 48:72]
-        stage[c, 89:113] = jnp.where((lane == LANES - 1)[None], high, low)
-        pu[phase_of[c], 1 - c, 0:64] = u[c][0]
-        pu[phase_of[c], 1 - c, 64:72] = e[c]
         moved = swap(jnp.where(odd[None], high, low), odd[None])
         mid = mid + jnp.where(edge[None], 0.0, moved)
         pq[phase_of[c], 1 - c, 0] = jnp.where(odd[None], low, mid)
         pq[phase_of[c], 1 - c, 1] = jnp.where(odd[None], mid, high)
-
-    def pack_step(i, held):
-        out = []
-        for c in range(2):
-            for half in range(2):
-                x = stage[c, half * 64 + i]
-                x = pltpu.roll(x, 2 * i + 1, axis=1)
-                out.append(jnp.where(lax.div(lane, 2) == i, x, held[2 * c + half]))
-        return tuple(out)
-
-    for c in range(2):
-        stage[c, 113:128] = jnp.zeros((15, 8, LANES), F32)
-    zero = jnp.zeros((8, LANES), F32)
-    packed = lax.fori_loop(0, 64, pack_step, (zero, zero, zero, zero), unroll=16)
+    for c in range(2):
+        low, high = stage[c, 0:24], stage[c, 48:72]
+        stage[c, 72:80] = u[c][0].reshape(8, 8, LANES)
+        stage[c, 80:81] = e[c][None]
+        stage[c, 81:89] = m[c][0].reshape(8, 8, LANES)
+        stage[c, 89:113] = jnp.where((lane == LANES - 1)[None], high, low)
     for c in range(2):
         for half in range(2):
-            pack[c, half] = packed[2 * c + half]
+            held = jnp.zeros((8, LANES), F32)
+            for i in range(min(64, N_PACK - 64 * half)):
+                x = pltpu.roll(stage[c, half * 64 + i], (2 * i + 1) % LANES, axis=1)
+                held = jnp.where((lane == 2 * i) | (lane == 2 * i + 1), x, held)
+            pack[c, half] = held
 
     pl.semaphore_wait(barrier, 4)
-
-    def copy(src, dst, sem, target):
-        return pltpu.make_async_remote_copy(
-            src_ref=src,
-            dst_ref=dst,
-            send_sem=send_sem.at[sem],
-            recv_sem=recv_sem.at[sem],
-            device_id=target,
-            device_id_type=MESH,
-        )
-
-    near_side, far_side = core, 1 - core
-    to_before = copy(pack, gy_in.at[1], 0, before)
-    to_after = copy(pack, gy_in.at[0], 1, after)
     to_before.start()
     to_after.start()
-    sends = {}
-    for name, phase, side, target, sem in (
-        ("far", 1, far_side, far, 2),
-        ("near", 0, near_side, near, 6),
-    ):
-        for i, buf in enumerate((pu, pq, pm)):
-            where = buf.at[phase, side]
-            sends[name, i] = copy(where, where, sem + i, target)
-            sends[name, i].start()
-        where = pe.at[phase, side]
-        sends[name, 3] = copy(where, where, sem + 3, target)
+    for key in ("potential", "low", "high"):
+        sends["far", key].start()
+    for key in ("potential", "low", "high", "mass"):
+        sends["near", key].start()
     to_before.wait()
     to_after.wait()
-    own_entry = (lane >= 2 * (N_HALO - 64))
+    own_entry = lane >= 2 * (N_HALO - 64)
     for c in range(2):
         for half in range(2):
             merged = jnp.where(even, gy_in[0, c, half], gy_in[1, c, half])
             if half == 1:
                 merged = jnp.where(own_entry, pack[c, half], merged)
             pe[phase_of[c], 1 - c, half] = merged
-    sends["near", 3].start()
-    sends["far", 3].start()
+    for key in ("edges", "mass"):
+        sends["far", key].start()
+    sends["near", "edges"].start()
 
     for phase, name in ((0, "near"), (1, "far")):
-        for i in range(4):
-            sends[name, i].wait()
+        sends[name, "potential"].wait()
+        sends[name, "edges"].wait()
         own_side = near_side if phase == 0 else far_side
 
-        def unpack_step(i, _):
-            for side in range(2):
-                for half in range(2):
-                    shift = LANES - (2 * i + 1)
-                    stage[side, half * 64 + i] = pltpu.roll(pe[phase, side, half], shift, axis=1)
-            return 0
-
-        lax.fori_loop(0, 64, unpack_step, 0, unroll=16)
-
+        for side in range(2):
+            for half in range(2):
+                x = pe[phase, side, half]
+                for i in range(min(64, N_PACK - 64 * half)):
+                    stage[side, half * 64 + i] = pltpu.roll(x, LANES - (2 * i + 1), axis=1)
+
+        u = [[pu[phase, s, 0:64], stage[s, 72:80].reshape(64, LANES)] for s in range(2)]
+        e = [[pu[phase, s, 64:72], stage[s, 80]] for s in range(2)]
+
+        def partners(x, mask, at_edge):
+            moved_main, moved_edge = swap(x[0], mask), swap(x[1], mask)
+            return [jnp.where(at_edge, moved_edge, moved_main), moved_main]
+
+        def beta_sums(u):
+            for s in range(2):
+                forward_sums(kf_ref, s_ref, s, u[s], partners(u[s], odd[0:1], edge[0:1]))
+
+        beta_sums(u)
+        sends[name, "low"].wait()
+        sends[name, "high"].wait()
         for chunk in range(4):
             sides = ((0,), (0, 1), (0, 1), (1,))[chunk]
 
@@ -448,25 +461,23 @@
             nu_ref[1, rows, :, outer] = swap(other, odd[None])
             nu_ref[2, rows, :, outer] = jnp.where(odd[None], swap(low, odd[None]), ep2)
 
-        u = [[pu[phase, s, 0:64], stage[s, 72:80].reshape(64, LANES)] for s in range(2)]
-        e = [[pu[phase, s, 64:72], stage[s, 80]] for s in range(2)]
-        m = [[pm[phase, s], stage[s, 81:89].reshape(64, LANES)] for s in range(2)]
         lam = [region_scale(nu_ref, lanes_at(g), odd) for g in range(2)]
 
-        def partners(x, mask, at_edge):
-            moved_main, moved_edge = swap(x[0], mask), swap(x[1], mask)
-            return [jnp.where(at_edge, moved_edge, moved_main), moved_main]
+        def masses():
+            return [[pm[phase, s], stage[s, 81:89].reshape(64, LANES)] for s in range(2)]
 
         for it in range(ITERS + 1):
-            for s in range(2):
-                forward_sums(kf_ref, s_ref, s, u[s], partners(u[s], odd[0:1], edge[0:1]))
             ep = [partners(e[s], odd, edge) for s in range(2)]
             weights = [
                 levels([e[0][g], e[1][g]], [ep[0][g], ep[1][g]], odd, lam[g]) for g in range(2)
             ]
             if it < ITERS:
-                u = backward(kb_ref, r_ref, s_ref, nu_ref, 2, weights, odd, m)
+                total = source_sums(kb_ref, r_ref, s_ref, nu_ref, 2, weights, odd)
+                if it == 0:
+                    sends[name, "mass"].wait()
+                u = new_potential(total, masses())
                 e = [[weights[g][4][s] for g in range(2)] for s in range(2)]
+                beta_sums(u)
 
         own_w, partner_w, _, final_w = weights[0][:4]
         own_col = 1 - own_side
@@ -535,8 +546,8 @@
             pltpu.VMEM(forward.shape, BF16),
             pltpu.VMEM(back.shape, BF16),
             pltpu.SemaphoreType.DMA((5,)),
-            pltpu.SemaphoreType.DMA((10,)),
-            pltpu.SemaphoreType.DMA((10,)),
+            pltpu.SemaphoreType.DMA((12,)),
+            pltpu.SemaphoreType.DMA((12,)),
         ],
         compiler_params=pltpu.CompilerParams(
             collective_id=0, has_side_effects=True, vmem_limit_bytes=56 * 2**20

time: 22 us -> 21.7 us (0.986)
  Pallas kernels: 21.2 us -> 20.9 us
    pallas_call x1, Pallas kernels: 20.4 us -> 20 us  [per_device(): pl.pallas_call(functools.partial(body, nx, ny), out_shape=(pltpu.VMEM(alp...]
where the time goes in v3:
time: 21.7 us; the launch traced here: 21.5 us
  Pallas kernels  20.9 us (96%)
  between operations  0.64 us (3%)
    pallas_call x1, Pallas kernels, per_device(): pl.pallas_call(functools.partial(body, nx, ny), out_shape=(pltpu.VMEM(alp...  20 us
    pallas_call x1, Pallas kernels, per_device(): pl.pallas_call(write_out, out_shape=tuple((jax.ShapeDtypeStruct(r.shape,...  0.86 us

profile of v3, /device:TPU:1, one launch (start us, length us, event | category | flops | bytes accessed | tf_op | source)
XLA Modules:
  0.0 21.5 jit_solution(3679251600466083515)
XLA Ops:
  0.6 20.0 %shard_map.68 = (f32[2,8,8,128]{3,2,1,0:T(8,128)S(1)}, f32[2,24,24,128]{3,2,1,0:T(8,128)S(1)}) custom-call(f32[2,8,8,128]{3,2,1,0:T(8,128)} %mass_hbm.1, f32[2,8,8,128]{3,2,1,0:T(8,128)} %alpha_hbm.1, f32[2,24,24,128]{3,2,1,0:T(8,128)} %part_hbm.1, bf16[576,192]{1,0:T(8,128)(2,1)} %constant.4.clone.kf_hbm, bf16[3,128,192]{2,1,0:T(8,128)(2,1)} %constant.5.clone.kb_hbm), custom_call_target="tpu_custom_call" | custom-call | tf_op jit(solution)/shard_map/pallas_call | solution.py:523
  20.7 0.9 %shard_map.69 = (f32[2,8,8,128]{3,2,1,0:T(8,128)}, f32[2,24,24,128]{3,2,1,0:T(8,128)}) custom-call(f32[2,8,8,128]{3,2,1,0:T(8,128)S(1)} %get-tuple-element.4.alpha_in, f32[2,24,24,128]{3,2,1,0:T(8,128)S(1)} %get-tuple-element.5.part_in), custom_call_target="tpu_custom_call" | custom-call | tf_op jit(solution)/shard_map/pallas_call | solution.py:560

commit v4 on v3

--- a/solution.py
+++ b/solution.py
@@ -233,6 +233,7 @@
     pe,
     pack,
     gy_in,
+    above,
     stage,
     s_ref,
     r_ref,
@@ -244,6 +245,7 @@
     kf_ref,
     kb_ref,
     load_sem,
+    ready_sem,
     send_sem,
     recv_sem,
 ):
@@ -255,7 +257,9 @@
     before = (gx, lax.rem(gy + ny - 1, ny))
     after = (gx, lax.rem(gy + 1, ny))
     barrier = pltpu.get_barrier_semaphore()
-    for target in (near, far, before, after):
+    near_before, near_after = (near[0], before[1]), (near[0], after[1])
+    far_before, far_after = (far[0], before[1]), (far[0], after[1])
+    for target in (near, far, before, near_before, far_before):
         pl.semaphore_signal(barrier, inc=1, device_id=target, device_id_type=MESH)
 
     loads = [
@@ -386,34 +390,46 @@
                 held = jnp.where((lane == 2 * i) | (lane == 2 * i + 1), x, held)
             pack[c, half] = held
 
-    pl.semaphore_wait(barrier, 4)
-    to_before.start()
+    pl.semaphore_wait(barrier, 5)
+    pl.semaphore_signal(ready_sem, inc=1, device_id=after, device_id_type=MESH)
     to_after.start()
+    across = [
+        copy(pack.at[1 - core], above.at[0, near_side], 12, near_after),
+        copy(pack.at[core], above.at[1, far_side], 13, far_after),
+    ]
+    across[1].start()
+    across[0].start()
     for key in ("potential", "low", "high"):
         sends["far", key].start()
     for key in ("potential", "low", "high", "mass"):
         sends["near", key].start()
+    pl.semaphore_wait(ready_sem, 1)
+    to_before.start()
     to_before.wait()
-    to_after.wait()
     own_entry = lane >= 2 * (N_HALO - 64)
     for c in range(2):
         for half in range(2):
-            merged = jnp.where(even, gy_in[0, c, half], gy_in[1, c, half])
+            merged = gy_in[1, c, half]
             if half == 1:
                 merged = jnp.where(own_entry, pack[c, half], merged)
             pe[phase_of[c], 1 - c, half] = merged
     for key in ("edges", "mass"):
         sends["far", key].start()
     sends["near", "edges"].start()
+    to_after.wait()
+    for c in range(2):
+        above[phase_of[c], 1 - c] = gy_in[0, c]
 
     for phase, name in ((0, "near"), (1, "far")):
         sends[name, "potential"].wait()
         sends[name, "edges"].wait()
+        across[phase].wait()
         own_side = near_side if phase == 0 else far_side
 
         for side in range(2):
             for half in range(2):
-                x = pe[phase, side, half]
+                from_above = even if half == 0 else even & (lane < 2 * (N_HALO - 64))
+                x = jnp.where(from_above, above[phase, side, half], pe[phase, side, half])
                 for i in range(min(64, N_PACK - 64 * half)):
                     stage[side, half * 64 + i] = pltpu.roll(x, LANES - (2 * i + 1), axis=1)
 
@@ -535,6 +551,7 @@
             pltpu.VMEM((2, 2, 2, 8, LANES), F32),
             pltpu.VMEM((2, 2, 8, LANES), F32),
             pltpu.VMEM((2, 2, 2, 8, LANES), F32),
+            pltpu.VMEM((2, 2, 2, 8, LANES), F32),
             pltpu.VMEM((2, 128, 8, LANES), F32),
             pltpu.VMEM((2, 3, 24, 8, 4 * LANES), F32),
             pltpu.VMEM((3, 32, 8, 4 * LANES), F32),
@@ -546,8 +563,9 @@
             pltpu.VMEM(forward.shape, BF16),
             pltpu.VMEM(back.shape, BF16),
             pltpu.SemaphoreType.DMA((5,)),
-            pltpu.SemaphoreType.DMA((12,)),
-            pltpu.SemaphoreType.DMA((12,)),
+            pltpu.SemaphoreType.REGULAR,
+            pltpu.SemaphoreType.DMA((14,)),
+            pltpu.SemaphoreType.DMA((14,)),
         ],
         compiler_params=pltpu.CompilerParams(
             collective_id=0, has_side_effects=True, vmem_limit_bytes=56 * 2**20

time: 21.7 us -> 21.3 us (0.982)
  Pallas kernels: 20.9 us -> 20.5 us
    pallas_call x1, Pallas kernels: 20 us -> 19.6 us  [per_device(): pl.pallas_call(functools.partial(body, nx, ny), out_shape=(pltpu.VMEM(alp...]
where the time goes in v4:
time: 21.3 us; the launch traced here: 21.1 us
  Pallas kernels  20.5 us (96%)
  between operations  0.64 us (3%)
    pallas_call x1, Pallas kernels, per_device(): pl.pallas_call(functools.partial(body, nx, ny), out_shape=(pltpu.VMEM(alp...  19.6 us
    pallas_call x1, Pallas kernels, per_device(): pl.pallas_call(write_out, out_shape=tuple((jax.ShapeDtypeStruct(r.shape,...  0.86 us

profile of v4, /device:TPU:1, one launch (start us, length us, event | category | flops | bytes accessed | tf_op | source)
XLA Modules:
  0.0 21.1 jit_solution(17269284911221144767)
XLA Ops:
  0.6 19.6 %shard_map.68 = (f32[2,8,8,128]{3,2,1,0:T(8,128)S(1)}, f32[2,24,24,128]{3,2,1,0:T(8,128)S(1)}) custom-call(f32[2,8,8,128]{3,2,1,0:T(8,128)} %mass_hbm.1, f32[2,8,8,128]{3,2,1,0:T(8,128)} %alpha_hbm.1, f32[2,24,24,128]{3,2,1,0:T(8,128)} %part_hbm.1, bf16[576,192]{1,0:T(8,128)(2,1)} %constant.4.clone.kf_hbm, bf16[3,128,192]{2,1,0:T(8,128)(2,1)} %constant.5.clone.kb_hbm), custom_call_target="tpu_custom_call" | custom-call | tf_op jit(solution)/shard_map/pallas_call | solution.py:539
  20.2 0.9 %shard_map.69 = (f32[2,8,8,128]{3,2,1,0:T(8,128)}, f32[2,24,24,128]{3,2,1,0:T(8,128)}) custom-call(f32[2,8,8,128]{3,2,1,0:T(8,128)S(1)} %get-tuple-element.4.alpha_in, f32[2,24,24,128]{3,2,1,0:T(8,128)S(1)} %get-tuple-element.5.part_in), custom_call_target="tpu_custom_call" | custom-call | tf_op jit(solution)/shard_map/pallas_call | solution.py:578
